TPU v7x, 128 devices: a whole 4x4x4 slice. The times are simulated.
128 devices in a mesh: fa: 8 (over z, x_hi), fb: 16 (over x_lo, y, core).
Axes of the slice: x: 4 (x_hi: 2, x_lo: 2; x = x_hi * 2 + x_lo), y: 4, z: 4, core: 2. Of those that a mesh axis runs over, the one named last changes fastest.
Arguments:
- view_a: bfloat16 [4096, 8192], P(('fa', 'fb')), may hold values from -300 to 300
- view_b: bfloat16 [4096, 8192], P(('fa', 'fb')), may hold values from -300 to 300
Outputs:
- loss: float32 [], replicated
- grad_a: bfloat16 [4096, 8192], P(('fa', 'fb'))
- grad_b: bfloat16 [4096, 8192], P(('fa', 'fb'))
All inputs are finite; a program needn't handle non-finite values.
Results may differ from a plain program's by a relative error of at most 0.04.
Values may be sent and summed in bfloat16 or wider, within the bound.
No kernel may reach another device: no remote copies, remote signals or barrier semaphores. Data moves between devices by JAX's collectives and lax.ppermute only.
A program may use at most 192 MiB of HBM per device.

v0:
```python
import jax
import jax.numpy as jnp
from jax import lax
from jax.sharding import PartitionSpec as P

off_weight = 0.0051
norm_eps = 1e-05


def moments(columns):
    values = columns.astype(jnp.float32)
    mean = jnp.mean(values, axis=0)
    centred = values - mean
    var = jnp.mean(centred * centred, axis=0)
    rstd = lax.rsqrt(var + norm_eps)
    return (centred * rstd, rstd)


def on_device(view_a, view_b):
    rows_dev = view_a.shape[0]
    features = view_a.shape[1]
    count_a = lax.axis_size("fa")
    count_b = lax.axis_size("fb")
    width_a = features // count_a
    width_b = features // count_b
    a_mixed = lax.all_to_all(view_a, "fa", split_axis=1, concat_axis=0, tiled=True)
    a_cols = lax.all_gather(
        a_mixed.reshape(1, count_a * rows_dev, width_a), "fb", axis=0, tiled=True
    ).reshape(-1, width_a)
    b_mixed = lax.all_to_all(view_b, "fb", split_axis=1, concat_axis=0, tiled=True)
    b_cols = lax.all_gather(
        b_mixed.reshape(count_b, 1, rows_dev, width_b), "fa", axis=1, tiled=True
    ).reshape(-1, width_b)
    batch = a_cols.shape[0]
    norm_a, rstd_a = moments(a_cols)
    norm_b, rstd_b = moments(b_cols)
    normed_a = norm_a.astype(jnp.bfloat16)
    normed_b = norm_b.astype(jnp.bfloat16)
    corr = (
        lax.dot_general(
            normed_a, normed_b, (((0,), (0,)), ((), ())), preferred_element_type=jnp.float32
        )
        / batch
    )
    row_ids = lax.axis_index("fa") * width_a + lax.broadcasted_iota(
        jnp.int32, (width_a, width_b), 0
    )
    col_ids = lax.axis_index("fb") * width_b + lax.broadcasted_iota(
        jnp.int32, (width_a, width_b), 1
    )
    diagonal = row_ids == col_ids
    missing = 1.0 - corr
    tile_loss = jnp.sum(jnp.where(diagonal, missing * missing, off_weight * corr * corr))
    gcorr = jnp.where(diagonal, -2.0 * missing, 2.0 * off_weight * corr).astype(jnp.bfloat16)
    loss = lax.psum(tile_loss, ("fa", "fb")) / features
    share_a = count_a * rows_dev
    place_a = lax.axis_index("fb") * share_a
    place_b = lax.axis_index("fa")
    a_norm_rows = lax.dynamic_slice_in_dim(norm_a, place_a, share_a, 0)
    b_norm_rows = lax.dynamic_slice_in_dim(
        norm_b.reshape(count_b, count_a, rows_dev, width_b), place_b, 1, 1
    ).reshape(-1, width_b)
    b_term = jnp.dot(normed_a, gcorr, preferred_element_type=jnp.float32)
    a_term = lax.dot_general(
        normed_b, gcorr, (((1,), (1,)), ((), ())), preferred_element_type=jnp.float32
    )
    a_full = lax.psum(a_term.astype(jnp.bfloat16), "fb").astype(jnp.float32)
    mean_ga = jnp.sum(a_full, axis=0) / batch
    mean_gna = jnp.sum(a_full * norm_a, axis=0) / batch
    a_grad_rows = lax.dynamic_slice_in_dim(a_full, place_a, share_a, 0)
    b_full = lax.psum(b_term.astype(jnp.bfloat16), "fa").astype(jnp.float32)
    mean_gb = jnp.sum(b_full, axis=0) / batch
    mean_gnb = jnp.sum(b_full * norm_b, axis=0) / batch
    b_grad_rows = lax.dynamic_slice_in_dim(
        b_full.reshape(count_b, count_a, rows_dev, width_b), place_b, 1, 1
    ).reshape(-1, width_b)
    a_out = (rstd_a * (a_grad_rows - mean_ga - a_norm_rows * mean_gna)).astype(jnp.bfloat16)
    b_out = (rstd_b * (b_grad_rows - mean_gb - b_norm_rows * mean_gnb)).astype(jnp.bfloat16)
    grad_a = lax.all_to_all(a_out, "fa", split_axis=0, concat_axis=1, tiled=True)
    grad_b = lax.all_to_all(b_out, "fb", split_axis=0, concat_axis=1, tiled=True)
    return (loss, grad_a, grad_b)


def solution(mesh):
    return jax.shard_map(
        on_device,
        mesh=mesh,
        in_specs=(P(("fa", "fb"), None), P(("fa", "fb"), None)),
        out_specs=(P(), P(("fa", "fb"), None), P(("fa", "fb"), None)),
        check_vma=False,
    )
```

profile of v0, /device:TPU:0, one launch (start us, length us, event | category | flops | bytes accessed | tf_op | source)
XLA Modules:
  0.0 630.7 jit_solution(12596799508733061439)
XLA Ops:
  7.2 0.0 all-gather.6.cloned.1.call-start
  7.2 1.1 copy.35
  8.3 16.4 %all_to_all.67 = bf16[32,16,512]{2,0,1:T(8,128)(2,1)} all-to-all(bf16[32,16,512]{2,0,1:T(8,128)(2,1)S(1)} %bitcast.67), channel_id=1, replica_groups=mesh['fa'=8,'fb'=16] {'fb'}, dimensions={1} | all-to-all | bytes 1048576 | tf_op jit(solution)/shard_map/all_to_all | solution.py:30
  24.7 0.0 all-gather.6.cloned.1.call-update
  24.7 0.0 all-gather.4.cloned.1.call-start
  24.7 1.1 copy.36
  25.8 23.4 %all_to_all.68 = bf16[32,8,1024]{2,0,1:T(8,128)(2,1)} all-to-all(bf16[32,8,1024]{2,0,1:T(8,128)(2,1)S(1)} %bitcast.68), channel_id=1, replica_groups=mesh['fa'=8,'fb'=16] {'fa'}, dimensions={1} | all-to-all | bytes 1048576 | tf_op jit(solution)/shard_map/all_to_all | solution.py:26
  49.2 0.0 all-gather.4.cloned.1.call-update
  49.2 0.0 all-reduce.3.cloned.1.call-start
  49.3 48.2 %all-gather.6.cloned.1.call-done = bf16[16,256,512]{2,1,0:T(8,128)(2,1)} async-done(((bf16[16,32,512]{2,1,0:T(8,128)(2,1)}), bf16[16,256,512]{2,1,0:T(8,128)(2,1)}) %all-gather.6.cloned.1.call-update) | async-done | bytes 4194320 | tf_op jit(solution)/shard_map/all_gather | solution.py:31
  97.4 0.0 copy-start.1
  97.4 3.0 convert_reduce_fusion.2
  100.4 3.3 multiply_reduce_fusion.3
  103.8 0.0 copy-done.1
  103.8 6.2 subtract_multiply_fusion
  110.0 3.1 fusion.4
  113.1 35.9 %all-gather.4.cloned.1.call-done = bf16[16,256,1024]{2,1,0:T(8,128)(2,1)} async-done(((bf16[1,256,1024]{2,1,0:T(8,128)(2,1)}), bf16[16,256,1024]{2,1,0:T(8,128)(2,1)}) %all-gather.4.cloned.1.call-update) | async-done | bytes 8388624 | tf_op jit(solution)/shard_map/all_gather | solution.py:27
  149.0 0.0 copy-start
  149.0 4.8 convert_reduce_fusion
  153.8 1.0 copy-done
  154.8 2.2 multiply_reduce_fusion.1
  157.0 0.0 copy-start.4
  157.0 9.3 %multiply_convert_fusion = bf16[16,256,1024]{2,1,0:T(8,128)(2,1)} fusion(bf16[16,256,1024]{2,1,0:T(8,128)(2,1)} %all-gather.4.cloned.1.call-done, f32[1024]{0:T(1024)S(1)} %add_rsqrt_fusion, f32[1024]{0:T(1024)S(1)} %broadcast_multiply_fusion.2), kind=kLoop, calls=%fused_computation.3 | loop fusion | flops 16777216 | bytes 16785408 | tf_op jit(solution)/shard_map/convert_element_type | solution.py:37
  166.4 0.0 copy-done.4
  166.4 8.0 %fusion.8 = (f32[]{:T(128)}, f32[1024,512]{1,0:T(8,128)S(1)}) fusion(s32[512]{0:T(512)S(1)} %iota_add_fusion.1, s32[1024]{0:T(1024)S(1)} %iota_add_fusion, bf16[4096,1024]{1,0:T(8,128)(2,1)} %bitcast.61, bf16[4096,512]{1,0:T(8,128)(2,1)S(1)} %bitcast.62), kind=kOutput, calls=%fused_computation.21 | convolution fusion | flops 4299161600 | bytes 14686212 | tf_op jit(solution)/shard_map/dot_general | solution.py:40
  174.4 0.0 copy-done.5
  174.4 7.4 %convolution_convert_fusion = bf16[4096,1024]{1,0:T(8,128)(2,1)} fusion(bf16[4096,512]{1,0:T(8,128)(2,1)S(1)} %copy-done.5, f32[1024,512]{1,0:T(8,128)S(1)} %get-tuple-element.11, s32[512]{0:T(512)S(1)} %iota_add_fusion.1, s32[1024]{0:T(1024)S(1)} %iota_add_fusion), kind=kOutput, calls=%fused_computation.14 | convolution fusion | flops 4302831616 | bytes 14686208 | tf_op jit(solution)/shard_map/dot_general | solution.py:64
  181.8 0.0 all-reduce.3.cloned.1.call-update
  181.8 0.0 all-reduce.5.cloned.1.call-start
  181.9 143.8 %all-reduce.3.cloned.1.call-done = bf16[4096,1024]{1,0:T(8,128)(2,1)} async-done(((bf16[4096,1024]{1,0:T(8,128)(2,1)}), bf16[4096,1024]{1,0:T(8,128)(2,1)}) %all-reduce.3.cloned.1.call-update) | async-done | bytes 8388624 | tf_op jit(solution)/shard_map/psum | solution.py:67
  325.7 12.8 %convert_reduce_fusion.1 = (f32[1024]{0:T(1024)S(1)}, f32[1024]{0:T(1024)S(1)}, f32[4096,1024]{1,0:T(8,128)}) fusion(bf16[4096,1024]{1,0:T(8,128)(2,1)} %all-reduce.3.cloned.1.call-done, f32[1024]{0:T(1024)S(1)} %add_rsqrt_fusion, f32[1024]{0:T(1024)S(1)} %broadcast_multiply_fusion.2, bf16[16,256,1024]{2,1,0:T(8,128)(2,1)} %all-gather.4.cloned.1.call-done), kind=kLoop, calls=%fused_computation.11 | loop fusion | flops 29358080 | bytes 33570816 | tf_op jit(solution)/shard_map/reduce_sum | solution.py:68
  338.4 12.1 %fusion.5 = bf16[4096,512]{1,0:T(8,128)(2,1)} fusion(f32[4096,1024]{1,0:T(8,128)} %get-tuple-element.7, f32[1024,512]{1,0:T(8,128)S(1)} %get-tuple-element.11, s32[512]{0:T(512)S(1)} %iota_add_fusion.1, s32[1024]{0:T(1024)S(1)} %iota_add_fusion), kind=kOutput, calls=%fused_computation.17 | convolution fusion | flops 4304928768 | bytes 23074816 | tf_op jit(solution)/shard_map/dot_general | solution.py:63
  350.5 0.0 all-reduce.5.cloned.1.call-update
  350.6 11.5 %convert_element_type.72 = f32[4096,1024]{1,0:T(8,128)} convert(bf16[4096,1024]{1,0:T(8,128)(2,1)} %all-reduce.3.cloned.1.call-done) | non-fusion elementwise | flops 4194304 | bytes 25165824 | tf_op jit(solution)/shard_map/convert_element_type | solution.py:67
  362.1 2.6 multiply_convert_fusion.1
  364.6 6.5 %all-to-all-start.2 = ((bf16[8,32,1024]{2,1,0:T(8,128)(2,1)}), bf16[8,32,1024]{2,1,0:T(8,128)(2,1)S(1)}, u32[]{:S(2)}, u32[]{:S(2)}) async-start(bf16[8,32,1024]{2,1,0:T(8,128)(2,1)} %bitcast.8), calls=%async_computation.2 | async-start | bytes 1048576 | tf_op jit(solution)/shard_map/all_to_all | solution.py:79
  371.2 170.6 %all-reduce.5.cloned.1.call-done = bf16[4096,512]{1,0:T(8,128)(2,1)} async-done(((bf16[4096,512]{1,0:T(8,128)(2,1)}), bf16[4096,512]{1,0:T(8,128)(2,1)}) %all-reduce.5.cloned.1.call-update) | async-done | bytes 4194320 | tf_op jit(solution)/shard_map/psum | solution.py:71
  541.8 3.5 convert.3
  545.3 0.0 copy-done.2
  545.3 1.2 copy-done.3
  546.5 2.1 convert_reduce_fusion.3
  548.6 2.3 fusion.12
  550.9 0.0 all-to-all-done.2
  550.9 4.4 all-to-all-start.3
  555.3 65.4 %psum.21 = f32[]{:T(128)} all-reduce(f32[]{:T(128)} %get-tuple-element.10), channel_id=1, replica_groups=mesh['fa'=8,'fb'=16] {'fa','fb'}, use_global_device_ids=true, to_apply=%region_5.6 | all-reduce | flops 1 | bytes 8 | tf_op jit(solution)/shard_map/psum | solution.py:55
  621.4 0.8 copy.31
  622.2 0.0 all-to-all-done.3
  622.2 0.8 copy.32
  (11 shorter events, 0.0 us)
Async XLA Ops:
  7.2 90.3 %all-gather.6.cloned.1.call-start = ((), (), s32[]{:S(2)}) async-start(), calls=%async_computation.7 | async-start | bytes 4718592 | tf_op jit(solution)/shard_map/all_gather | solution.py:31
  24.7 124.3 %all-gather.4.cloned.1.call-start = ((), (), s32[]{:S(2)}) async-start(), calls=%async_computation.4 | async-start | bytes 8912896 | tf_op jit(solution)/shard_map/all_gather | solution.py:27
  49.2 276.5 %all-reduce.3.cloned.1.call-start = ((), (), s32[]{:S(2)}) async-start(), calls=%async_computation.5 | async-start | bytes 16777216 | tf_op jit(solution)/shard_map/psum | solution.py:67
  97.4 6.3 %copy-start.1 = (bf16[16,256,512]{2,1,0:T(8,128)(2,1)S(1)}, bf16[16,256,512]{2,1,0:T(8,128)(2,1)}, u32[]{:S(2)}) copy-start(bf16[16,256,512]{2,1,0:T(8,128)(2,1)} %all-gather.6.cloned.1.call-done) | copy-start | bytes 12582916
  149.0 5.8 copy-start
  157.0 9.3 %copy-start.4 = (bf16[16,8,32,512]{3,2,1,0:T(8,128)(2,1)S(1)}, bf16[16,8,32,512]{3,2,1,0:T(8,128)(2,1)}, u32[]{:S(2)}) copy-start(bf16[16,8,32,512]{3,2,1,0:T(8,128)(2,1)} %get-tuple-element.9) | copy-start | bytes 12582916
  166.4 8.0 %copy-start.5 = (bf16[4096,512]{1,0:T(8,128)(2,1)S(1)}, bf16[4096,512]{1,0:T(8,128)(2,1)}, u32[]{:S(2)}) copy-start(bf16[4096,512]{1,0:T(8,128)(2,1)} %fusion.4) | copy-start | bytes 12582916
  181.8 359.9 %all-reduce.5.cloned.1.call-start = ((), (), s32[]{:S(2)}) async-start(), calls=%async_computation.6 | async-start | bytes 8388608 | tf_op jit(solution)/shard_map/psum | solution.py:71
  364.6 186.3 %all-to-all-start.2 = ((bf16[8,32,1024]{2,1,0:T(8,128)(2,1)}), bf16[8,32,1024]{2,1,0:T(8,128)(2,1)S(1)}, u32[]{:S(2)}, u32[]{:S(2)}) async-start(bf16[8,32,1024]{2,1,0:T(8,128)(2,1)} %bitcast.8), calls=%async_computation.2 | async-start | bytes 1048576 | tf_op jit(solution)/shard_map/all_to_all | solution.py:79
  541.8 3.5 copy-start.2
  541.8 4.7 copy-start.3
  550.9 71.3 %all-to-all-start.3 = ((bf16[16,32,512]{2,1,0:T(8,128)(2,1)}), bf16[16,32,512]{2,1,0:T(8,128)(2,1)S(1)}, u32[]{:S(2)}, u32[]{:S(2)}) async-start(bf16[16,32,512]{2,1,0:T(8,128)(2,1)} %fusion.12), calls=%async_computation.3 | async-start | bytes 1048576 | tf_op jit(solution)/shard_map/all_to_all | solution.py:80
Sparse Core Ops, SparseCore 0:
  24.8 72.5 all-gather.5
  99.1 49.8 all-gather.3
  182.0 143.6 all-reduce.2
  350.7 191.0 all-reduce.4
where the time goes:
time: 632 us; the launch traced here: 631 us
  waiting for transfers between devices  399 us (63%)
  blocking collectives  105 us (17%)
  other arithmetic  66.8 us (11%)
  matrix products  27.5 us (4%)
  between operations  15.6 us (2%)
  starting transfers between devices  11.1 us (2%)
    psum x1, waiting for transfers between devices, on_device(): b_full = lax.psum(b_term.astype(jnp.bfloat16), 'fa').astype(jnp.float32)  171 us
    psum x1, waiting for transfers between devices, on_device(): a_full = lax.psum(a_term.astype(jnp.bfloat16), 'fb').astype(jnp.float32)  144 us
    psum x1, blocking collectives, on_device(): loss = lax.psum(tile_loss, ('fa', 'fb')) / features  65.4 us
    all_gather x1, waiting for transfers between devices, on_device(): lax.all_gather(b_mixed.reshape(count_b, 1, rows_dev, width_b), 'fa', axis...  48.2 us
    all_gather x1, waiting for transfers between devices, on_device(): lax.all_gather(a_mixed.reshape(1, count_a * rows_dev, width_a), 'fb', axi...  35.9 us
    all_to_all x1, blocking collectives, on_device(): lax.all_to_all(view_a, 'fa', split_axis=1, concat_axis=0, tiled=True)  23.4 us
    all_to_all x1, blocking collectives, on_device(): lax.all_to_all(view_b, 'fb', split_axis=1, concat_axis=0, tiled=True)  16.4 us
    reduce_sum x1, other arithmetic, on_device(): mean_ga = jnp.sum(a_full, axis=0) / batch  12.8 us
  transfers between devices with their start and end apart: 6, of which 4 were waited for; matrix products, arithmetic and copies ran while one was open for 6% of the time, Pallas kernels for 0%

commit v1 on v0

v1 whole, which is shorter than its diff:
```python
import functools

import jax
import jax.numpy as jnp
from jax import lax
from jax.experimental import pallas as pl
from jax.experimental.pallas import tpu as pltpu
from jax.sharding import Mesh, PartitionSpec as P

off_weight = 0.0051
norm_eps = 1e-05
bf16 = jnp.bfloat16
f32 = jnp.float32
axes = ("z", "xh", "xl", "y", "c")
chips = ("z", "xh", "xl", "y")
lanes = 128


def call(kernel, out_shape, *args, scratch=(), flops=0):
    one = isinstance(out_shape, jax.ShapeDtypeStruct)
    outs = [out_shape] if one else list(out_shape)
    moved = sum(a.size * a.dtype.itemsize for a in list(args) + outs)
    vmem = pl.BlockSpec(memory_space=pltpu.VMEM)
    return pl.pallas_call(
        kernel,
        out_shape=out_shape,
        in_specs=[vmem] * len(args),
        out_specs=vmem if one else [vmem] * len(outs),
        scratch_shapes=list(scratch),
        compiler_params=pltpu.CompilerParams(vmem_limit_bytes=48 * 2**20),
        cost_estimate=pl.CostEstimate(flops=flops, bytes_accessed=moved, transcendentals=0),
    )(*args)


def shape(dims, dtype):
    return jax.ShapeDtypeStruct(dims, dtype)


def shift(x, axis, step):
    n = lax.axis_size(axis)
    return lax.ppermute(x, axis, [(i, (i + step) % n) for i in range(n)])


def swap(x, axis, bit):
    return lax.ppermute(x, axis, [(i, i ^ bit) for i in range(lax.axis_size(axis))])


def stats_kernel(x_ref, out_ref):
    x = x_ref[...].astype(f32)
    mean = jnp.mean(x, axis=0, keepdims=True)
    centred = x - mean
    m2 = jnp.sum(centred * centred, axis=0, keepdims=True)
    width = x.shape[1]
    out_ref[...] = jnp.concatenate([mean, m2, jnp.zeros((6, width), f32)], axis=0)


def merge_stats(mine, other, rows):
    delta = other[0:1] - mine[0:1]
    mean = 0.5 * (mine[0:1] + other[0:1])
    var = (mine[1:2] + other[1:2]) / (2 * rows) + 0.25 * delta * delta
    return mean, lax.rsqrt(var + norm_eps)


def norm_kernel(x_ref, mine_ref, other_ref, a_ref, b_ref, diag_ref):
    rows = x_ref.shape[0]
    mean, rstd = merge_stats(mine_ref[...], other_ref[...], rows)
    norm = ((x_ref[...].astype(f32) - mean) * rstd).astype(bf16)
    a = norm[:, :lanes]
    b = norm[:, lanes:]
    a_ref[...] = a
    b_ref[...] = b
    diag = jnp.sum(a.astype(f32) * b.astype(f32), axis=0, keepdims=True)
    diag_ref[...] = jnp.broadcast_to(diag, diag_ref.shape)


def corr_kernel(*refs):
    a, b, out_ref, a_t = refs[:8], refs[8:16], refs[16], refs[17]
    rows = a[0].shape[0]
    for i in range(8):
        a_t[i * lanes : (i + 1) * lanes, :] = a[i][...].T
    for q in range(4):
        right = jnp.concatenate([b[2 * q][...], b[2 * q + 1][...]], axis=1)
        for p in range(4):
            here = pl.ds(p * 256, 256)
            out_ref[here, q * 256 : (q + 1) * 256] = jnp.dot(
                a_t[here, :], right, preferred_element_type=f32
            ).astype(bf16)


def grad_blocks(b, g_ref, outs, pair, transposed):
    rows = b[0].shape[0]
    cols = slice(pair * 256, (pair + 1) * 256)
    step = 256
    for r in range(0, rows, step):
        left = jnp.concatenate([v[r : r + step, :] for v in b], axis=1)
        if transposed:
            out = lax.dot_general(
                left, g_ref[cols, :], (((1,), (1,)), ((), ())), preferred_element_type=f32
            )
        else:
            out = jnp.dot(left, g_ref[:, cols], preferred_element_type=f32)
        out = out.astype(bf16)
        outs[0][r : r + step, :] = out[:, :lanes]
        outs[1][r : r + step, :] = out[:, lanes:]


def first_kernel(batch, *refs):
    a, b = refs[:8], refs[8:16]
    mine, other, diag_mine, diag_other = refs[16:20]
    g_ref, loss_ref, diag_ref = refs[20:23]
    ga, gb = refs[23:25], refs[25:27]
    size = mine.shape[0]
    diag = (diag_mine[...] + diag_other[...]) / batch
    diag_ref[...] = diag
    first = lax.broadcasted_iota(jnp.int32, (8, lanes), 0) == 0
    missing = 1.0 - diag
    total = jnp.where(first, missing * missing, 0.0)
    step = 128
    for r in range(0, size, step):
        corr = (mine[r : r + step, :].astype(f32) + other[r : r + step, :].astype(f32)) / batch
        if r == 0:
            ids = lax.broadcasted_iota(jnp.int32, (step, size), 0)
            corr = jnp.where(ids == lax.broadcasted_iota(jnp.int32, (step, size), 1), 0.0, corr)
        g_ref[r : r + step, :] = (2.0 * off_weight * corr).astype(bf16)
        square = jnp.sum((off_weight * corr * corr).reshape(step // 8, 8, size), axis=0)
        total = total + sum(square[:, c : c + lanes] for c in range(0, size, lanes))
    loss_ref[...] = total
    grad_blocks(b, g_ref, ga, 3, True)
    grad_blocks(a, g_ref, gb, 3, False)


def rest_kernel(*refs):
    a, b, g_ref = refs[:8], refs[8:16], refs[16]
    outs = refs[17:]
    ga, gb = outs[:6], outs[6:]
    for pair in (2, 1, 0):
        grad_blocks(b, g_ref, ga[2 * pair : 2 * pair + 2], pair, True)
        grad_blocks(a, g_ref, gb[2 * pair : 2 * pair + 2], pair, False)


def add_kernel(*refs):
    n = len(refs) // 3
    for i in range(n):
        x, y, out = refs[2 * i], refs[2 * i + 1], refs[2 * n + i]
        out[...] = (x[...].astype(f32) + y[...].astype(f32)).astype(bf16)


def add3_kernel(*refs):
    n = len(refs) // 4
    for i in range(n):
        x, y, z, out = refs[3 * i], refs[3 * i + 1], refs[3 * i + 2], refs[3 * n + i]
        out[...] = (x[...].astype(f32) + y[...].astype(f32) + z[...].astype(f32)).astype(bf16)


def sums_kernel(x_ref, mine_ref, other_ref, diag_ref, *refs):
    parts_a, parts_b = refs[:4], refs[4:8]
    full_ref, sums_ref = refs[8:]
    rows = x_ref.shape[0]
    mean, rstd = merge_stats(mine_ref[...], other_ref[...], rows)
    norm = (x_ref[...].astype(f32) - mean) * rstd
    rounded = norm.astype(bf16).astype(f32)
    coef = -2.0 * (1.0 - diag_ref[0:1, :])
    ga = sum(p[...].astype(f32) for p in parts_a) + coef * rounded[:, lanes:]
    gb = sum(p[...].astype(f32) for p in parts_b) + coef * rounded[:, :lanes]
    full = jnp.concatenate([ga, gb], axis=1)
    full_ref[...] = full
    s1 = jnp.sum(full, axis=0, keepdims=True)
    s2 = jnp.sum(full * norm, axis=0, keepdims=True)
    sums_ref[...] = jnp.concatenate([s1, s2, jnp.zeros((6, 2 * lanes), f32)], axis=0)


def final_kernel(x_ref, mine_ref, other_ref, full_ref, s_mine, s_other, out_ref):
    rows = x_ref.shape[0]
    mean, rstd = merge_stats(mine_ref[...], other_ref[...], rows)
    norm = (x_ref[...].astype(f32) - mean) * rstd
    sums = (s_mine[...] + s_other[...]) / (2 * rows)
    out_ref[...] = (rstd * (full_ref[...] - sums[0:1] - norm * sums[1:2])).astype(bf16)


def gather(own, ring, pair):
    across = shift(own, pair, 1)
    left = shift(own, ring, 1)
    right = shift(own, ring, -1)
    across_left = shift(across, ring, 1)
    opposite = shift(right, ring, -1)
    across_right = shift(across, ring, -1)
    across_opposite = shift(across_left, ring, 1)
    return [own, across, left, across_left, right, across_right, opposite, across_opposite]


def on_device(view_a, view_b):
    rows_dev, features = view_a.shape
    groups = features // lanes
    rows = rows_dev * groups
    batch = 2 * rows
    block = shape((rows, lanes), bf16)

    def split(view):
        return view.reshape(rows_dev, groups, lanes).transpose(1, 0, 2)

    both = jnp.concatenate([split(view_a), split(view_b)], axis=2)
    x = lax.all_to_all(both, chips, 0, 0, tiled=True).reshape(rows, 2 * lanes)
    mine = call(stats_kernel, shape((8, 2 * lanes), f32), x)
    other = shift(mine, "c", 1)
    own_a, own_b, diag_mine = call(
        norm_kernel, (block, block, shape((8, lanes), f32)), x, mine, other
    )
    diag_other = shift(diag_mine, "c", 1)
    a = gather(own_a, "y", "xl")
    b = gather(own_b, "z", "xh")
    size = 8 * lanes
    work = 2 * rows * size * size
    corr_mine = call(
        corr_kernel,
        shape((size, size), bf16),
        *a,
        *b,
        scratch=[pltpu.VMEM((size, rows), bf16)],
        flops=work,
    )
    corr_other = shift(corr_mine, "c", 1)
    g, loss, diag, a_o, a_xo, b_o, b_xo = call(
        functools.partial(first_kernel, batch),
        (shape((size, size), bf16), shape((8, lanes), f32), shape((8, lanes), f32))
        + (block,) * 4,
        *a,
        *b,
        corr_mine,
        corr_other,
        diag_mine,
        diag_other,
        flops=work // 2,
    )
    a_r1, a_r2 = shift(a_o, "y", 1), shift(a_xo, "y", -1)
    b_r1, b_r2 = shift(b_o, "z", 1), shift(b_xo, "z", -1)
    rest = call(rest_kernel, (block,) * 12, *a, *b, g, flops=work * 3 // 2)
    a_p, a_q, a_l, a_xl, a_r, a_xr = rest[:6]
    b_p, b_q, b_l, b_xl, b_r, b_xr = rest[6:]
    a_xr_in, b_xr_in = shift(a_xr, "y", 1), shift(b_xr, "z", 1)
    a_xl, b_xl = call(add_kernel, (block,) * 2, a_xl, a_r2, b_xl, b_r2)
    a_xl_in, b_xl_in = shift(a_xl, "y", -1), shift(b_xl, "z", -1)
    a_r, b_r = call(add_kernel, (block,) * 2, a_r, a_r1, b_r, b_r1)
    a_r_in, b_r_in = shift(a_r, "y", 1), shift(b_r, "z", 1)
    a_l_in, b_l_in = shift(a_l, "y", -1), shift(b_l, "z", -1)
    a_q, b_q = call(add3_kernel, (block,) * 2, a_q, a_xr_in, a_xl_in, b_q, b_xr_in, b_xl_in)
    a_q_in, b_q_in = shift(a_q, "xl", 1), shift(b_q, "xh", 1)
    full, s_mine = call(
        sums_kernel,
        (shape((rows, 2 * lanes), f32), shape((8, 2 * lanes), f32)),
        x,
        mine,
        other,
        diag,
        a_p,
        a_r_in,
        a_l_in,
        a_q_in,
        b_p,
        b_r_in,
        b_l_in,
        b_q_in,
    )
    s_other = shift(s_mine, "c", 1)
    out = call(
        final_kernel, shape((rows, 2 * lanes), bf16), x, mine, other, full, s_mine, s_other
    )
    back = lax.all_to_all(out.reshape(groups, rows_dev, 2 * lanes), chips, 0, 0, tiled=True)
    grad_a = back[:, :, :lanes].transpose(1, 0, 2).reshape(rows_dev, features)
    grad_b = back[:, :, lanes:].transpose(1, 0, 2).reshape(rows_dev, features)
    for axis, bit in (("xl", 1), ("xh", 1), ("y", 1), ("y", 2), ("z", 1), ("z", 2)):
        loss = loss + swap(loss, axis, bit)
    return (jnp.sum(loss) / features, grad_a, grad_b)


def solution(mesh):
    split = Mesh(mesh.devices.reshape(4, 2, 2, 4, 2), axes)
    return jax.shard_map(
        on_device,
        mesh=split,
        in_specs=(P(axes, None), P(axes, None)),
        out_specs=(P(), P(axes, None), P(axes, None)),
        check_vma=False,
    )
```

time: 632 us -> 224 us (0.35)
  waiting for transfers between devices: 399 us -> 98 us
  blocking collectives: 105 us -> 30 us
  other arithmetic: 66.8 us -> 0.76 us
  starting transfers between devices: 11.1 us -> 52.4 us
  Pallas kernels: 0 us -> 31.8 us
  matrix products: 27.5 us -> 0 us
  between operations: 15.6 us -> 2.66 us
    psum x2 -> x0, waiting for transfers between devices: 314 us -> none  [the longest x1 171 us: on_device(): b_full = lax.psum(b_term.astype(jnp.bfloat16), 'fa').astype(jnp.float32)]
    ppermute x0 -> x38, waiting for transfers between devices: none -> 98 us  [the longest x32 75.6 us: shift(): return lax.ppermute(x, axis, [(i, (i + step) % n) for i in range(n)])]
    all_gather x2 -> x0, waiting for transfers between devices: 84.1 us -> none  [the longest x1 48.2 us: on_device(): lax.all_gather(b_mixed.reshape(count_b, 1, rows_dev, width_b), 'fa', axis...]
    psum x1 -> x0, blocking collectives: 65.4 us -> none  [on_device(): loss = lax.psum(tile_loss, ('fa', 'fb')) / features]
    ppermute x0 -> x38, starting transfers between devices: none -> 45.5 us  [the longest x32 32.2 us: shift(): return lax.ppermute(x, axis, [(i, (i + step) % n) for i in range(n)])]
    pallas_call x0 -> x10, Pallas kernels: none -> 31.8 us  [call(): pl.pallas_call(kernel, out_shape=out_shape, in_specs=[vmem] * len(args),...]
    convert_element_type x5 -> x0, other arithmetic: 28.8 us -> none  [the longest x1 11.5 us: on_device(): a_full = lax.psum(a_term.astype(jnp.bfloat16), 'fb').astype(jnp.float32)]
    reduce_sum x6 -> x1, other arithmetic: 28.1 us -> 0.6 us  [on_device(): return (jnp.sum(loss) / features, grad_a, grad_b)]
  transfers between devices with their start and end apart: 6 -> 39, of which waited for: 4 -> 23; matrix products, arithmetic and copies ran while one was open for 6% -> 0% of each run, Pallas kernels for 0% -> 5%
where the time goes in v1:
time: 224 us
  waiting for transfers between devices  98 us (44%)
  starting transfers between devices  52.4 us (23%)
  Pallas kernels  31.8 us (14%)
  blocking collectives  30 us (13%)
  local copies, waits for them, and re-layouts  8.03 us (4%)
  between operations  2.66 us (1%)
    ppermute x32, waiting for transfers between devices, shift(): return lax.ppermute(x, axis, [(i, (i + step) % n) for i in range(n)])  75.6 us
    ppermute x32, starting transfers between devices, shift(): return lax.ppermute(x, axis, [(i, (i + step) % n) for i in range(n)])  32.2 us
    pallas_call x10, Pallas kernels, call(): pl.pallas_call(kernel, out_shape=out_shape, in_specs=[vmem] * len(args),...  31.8 us
    all_to_all x1, blocking collectives, on_device(): x = lax.all_to_all(both, chips, 0, 0, tiled=True).reshape(rows, 2 * lanes)  30 us
    ppermute x6, waiting for transfers between devices, swap(): lax.ppermute(x, axis, [(i, i ^ bit) for i in range(lax.axis_size(axis))])  22.4 us
    ppermute x6, starting transfers between devices, swap(): lax.ppermute(x, axis, [(i, i ^ bit) for i in range(lax.axis_size(axis))])  13.3 us
    all_to_all x1, starting transfers between devices, on_device(): lax.all_to_all(out.reshape(groups, rows_dev, 2 * lanes), chips, 0, 0, til...  6.88 us
    unnamed x39, local copies, waits for them, and re-layouts  5.04 us
  transfers between devices with their start and end apart: 39, of which 23 were waited for; matrix products, arithmetic and copies ran while one was open for 0% of the time, Pallas kernels for 5%

profile of v1, /device:TPU:0, one launch (start us, length us, event | category | flops | bytes accessed | tf_op | source)
XLA Modules:
  0.0 223.7 jit_solution(6073216368937472388)
XLA Ops:
  0.6 1.0 copy-done
  1.7 1.2 bitcast_bitcast_fusion
  3.1 30.0 %all_to_all.10 = bf16[64,32,256]{2,1,0:T(8,128)(2,1)S(1)} all-to-all(bf16[64,32,256]{2,1,0:T(8,128)(2,1)S(1)} %pad_maximum_fusion), channel_id=1, replica_groups=mesh['z'=4,'xh'=2,'xl'=2,'y'=4,'c'=2] {'z','xh','xl','y'}, dimensions={0} | all-to-all | bytes 2097152 | tf_op jit(solution)/shard_map/all_to_all | solution.py:202
  33.8 1.2 collective-permute-done.other_ref
  36.7 2.7 %collective-permute-start.4 = (bf16[2048,128]{1,0:T(8,128)(2,1)S(1)}, bf16[2048,128]{1,0:T(8,128)(2,1)S(1)}, u32[]{:S(2)}, u32[]{:S(2)}) collective-permute-start(bf16[2048,128]{1,0:T(8,128)(2,1)S(1)} %get-tuple-element.33.refs_0_), channel_id=1, source_target_pairs={{0,6},{2,0},{4,2},{6,4},{1,7},{3,1},{5,3},{7,5},{8,14},{10,8},{12,... | collective-permute-start | bytes 1572872 | tf_op jit(solution)/shard_map/ppermute | solution.py:41
  39.3 1.4 collective-permute-start.8
  40.8 9.5 %collective-permute-done.1.refs_1_ = bf16[2048,128]{1,0:T(8,128)(2,1)S(1)} collective-permute-done((bf16[2048,128]{1,0:T(8,128)(2,1)S(1)}, bf16[2048,128]{1,0:T(8,128)(2,1)S(1)}, u32[]{:S(2)}, u32[]{:S(2)}) %collective-permute-start.1) | collective-permute-done | bytes 524320 | tf_op jit(solution)/shard_map/ppermute | solution.py:41
  51.8 2.5 %collective-permute-start.5 = (bf16[2048,128]{1,0:T(8,128)(2,1)S(1)}, bf16[2048,128]{1,0:T(8,128)(2,1)S(1)}, u32[]{:S(2)}, u32[]{:S(2)}) collective-permute-start(bf16[2048,128]{1,0:T(8,128)(2,1)S(1)} %collective-permute-done.1.refs_1_), channel_id=1, source_target_pairs={{0,6},{2,0},{4,2},{6,4},{1,7},{3,1},{5,3},{7,5},{8,14},{10,8},{12,... | collective-permute-start | bytes 1572872 | tf_op jit(solution)/shard_map/ppermute | solution.py:41
  54.3 6.5 %collective-permute-done.8.refs_9_ = bf16[2048,128]{1,0:T(8,128)(2,1)S(1)} collective-permute-done((bf16[2048,128]{1,0:T(8,128)(2,1)S(1)}, bf16[2048,128]{1,0:T(8,128)(2,1)S(1)}, u32[]{:S(2)}, u32[]{:S(2)}) %collective-permute-start.8) | collective-permute-done | bytes 524320 | tf_op jit(solution)/shard_map/ppermute | solution.py:41
  60.8 3.2 %collective-permute-start.12 = (bf16[2048,128]{1,0:T(8,128)(2,1)S(1)}, bf16[2048,128]{1,0:T(8,128)(2,1)S(1)}, u32[]{:S(2)}, u32[]{:S(2)}) collective-permute-start(bf16[2048,128]{1,0:T(8,128)(2,1)S(1)} %collective-permute-done.8.refs_9_), channel_id=1, source_target_pairs={{0,96},{32,0},{64,32},{96,64},{1,97},{33,1},{65,33},{97,65},{2,98}... | collective-permute-start | bytes 1572872 | tf_op jit(solution)/shard_map/ppermute | solution.py:41
  64.0 1.3 collective-permute-start.6
  66.7 8.5 %collective-permute-done.10.refs_11_ = bf16[2048,128]{1,0:T(8,128)(2,1)S(1)} collective-permute-done((bf16[2048,128]{1,0:T(8,128)(2,1)S(1)}, bf16[2048,128]{1,0:T(8,128)(2,1)S(1)}, u32[]{:S(2)}, u32[]{:S(2)}) %collective-permute-start.10) | collective-permute-done | bytes 524320 | tf_op jit(solution)/shard_map/ppermute | solution.py:41
  75.1 1.5 collective-permute-done.6.refs_6_
  76.6 9.0 %collective-permute-done.13.refs_14_ = bf16[2048,128]{1,0:T(8,128)(2,1)S(1)} collective-permute-done((bf16[2048,128]{1,0:T(8,128)(2,1)S(1)}, bf16[2048,128]{1,0:T(8,128)(2,1)S(1)}, u32[]{:S(2)}, u32[]{:S(2)}) %collective-permute-start.13) | collective-permute-done | bytes 524320 | tf_op jit(solution)/shard_map/ppermute | solution.py:41
  85.6 2.9 %collective-permute-done.14.refs_15_ = bf16[2048,128]{1,0:T(8,128)(2,1)S(1)} collective-permute-done((bf16[2048,128]{1,0:T(8,128)(2,1)S(1)}, bf16[2048,128]{1,0:T(8,128)(2,1)S(1)}, u32[]{:S(2)}, u32[]{:S(2)}) %collective-permute-start.14) | collective-permute-done | bytes 524320 | tf_op jit(solution)/shard_map/ppermute | solution.py:41
  89.4 7.6 %shard_map.51.refs_16_ = bf16[1024,1024]{1,0:T(8,128)(2,1)} custom-call(bf16[2048,128]{1,0:T(8,128)(2,1)S(1)} %get-tuple-element.33.refs_0_, bf16[2048,128]{1,0:T(8,128)(2,1)S(1)} %collective-permute-done.1.refs_1_, bf16[2048,128]{1,0:T(8,128)(2,1)S(1)} %collective-permute-done.2.refs_2_, bf16[2048,128]{1,0:T(8,128)(2,1)S(1)} %collective-permute-done.3.refs_3_, ...), custom_call_target="tpu_custom_call" | custom-call | flops 4294967296 | bytes 10485760 | tf_op jit(solution)/shard_map/pallas_call | solution.py:24
  97.6 3.4 %collective-permute-done.16.refs_19_ = f32[8,128]{1,0:T(8,128)S(1)} collective-permute-done((f32[8,128]{1,0:T(8,128)S(1)}, f32[8,128]{1,0:T(8,128)S(1)}, u32[]{:S(2)}, u32[]{:S(2)}) %collective-permute-start.16) | collective-permute-done | bytes 4128 | tf_op jit(solution)/shard_map/ppermute | solution.py:41
  101.6 1.4 copy-done.13
  102.9 7.5 %shard_map.52 = (bf16[1024,1024]{1,0:T(8,128)(2,1)}, f32[8,128]{1,0:T(8,128)S(1)}, f32[8,128]{1,0:T(8,128)S(1)}, bf16[2048,128]{1,0:T(8,128)(2,1)S(1)}, bf16[204...) custom-call(bf16[2048,128]{1,0:T(8,128)(2,1)S(1)} %get-tuple-element.33.refs_0_, ...), custom_call_target="tpu_custom_call" | custom-call | flops 2147483648 | bytes 16793600 | tf_op jit(solution)/shard_map/pallas_call | solution.py:24
  110.9 2.7 %collective-permute-start.28 = (bf16[2048,128]{1,0:T(8,128)(2,1)S(1)}, bf16[2048,128]{1,0:T(8,128)(2,1)S(1)}, u32[]{:S(2)}, u32[]{:S(2)}) collective-permute-start(bf16[2048,128]{1,0:T(8,128)(2,1)S(1)} %get-tuple-element.49), channel_id=1, source_target_pairs={{0,6},{2,0},{4,2},{6,4},{1,7},{3,1},{5,3},{7,5},{8,14},{10,8},{12,... | collective-permute-start | bytes 1572872 | tf_op jit(solution)/shard_map/ppermute | solution.py:41
  113.6 3.2 %collective-permute-start.29 = (bf16[2048,128]{1,0:T(8,128)(2,1)S(1)}, bf16[2048,128]{1,0:T(8,128)(2,1)S(1)}, u32[]{:S(2)}, u32[]{:S(2)}) collective-permute-start(bf16[2048,128]{1,0:T(8,128)(2,1)S(1)} %get-tuple-element.51), channel_id=1, source_target_pairs={{0,96},{32,0},{64,32},{96,64},{1,97},{33,1},{65,33},{97,65},{2,98}... | collective-permute-start | bytes 1572872 | tf_op jit(solution)/shard_map/ppermute | solution.py:41
  116.9 10.8 %shard_map.53 = (bf16[2048,128]{1,0:T(8,128)(2,1)S(1)}, bf16[2048,128]{1,0:T(8,128)(2,1)S(1)}, bf16[2048,128]{1,0:T(8,128)(2,1)S(1)}, bf16[2048,128]{1,0:T(8,128...) custom-call(bf16[2048,128]{1,0:T(8,128)(2,1)} %copy-done.2, ...), custom_call_target="tpu_custom_call" | custom-call | flops 6442450944 | bytes 16777216 | tf_op jit(solution)/shard_map/pallas_call | solution.py:24
  128.1 3.2 %collective-permute-start.30 = (bf16[2048,128]{1,0:T(8,128)(2,1)S(1)}, bf16[2048,128]{1,0:T(8,128)(2,1)S(1)}, u32[]{:S(2)}, u32[]{:S(2)}) collective-permute-start(bf16[2048,128]{1,0:T(8,128)(2,1)S(1)} %get-tuple-element.52), channel_id=1, source_target_pairs={{0,6},{2,0},{4,2},{6,4},{1,7},{3,1},{5,3},{7,5},{8,14},{10,8},{12,... | collective-permute-start | bytes 1572872 | tf_op jit(solution)/shard_map/ppermute | solution.py:41
  131.3 3.2 %collective-permute-start.32 = (bf16[2048,128]{1,0:T(8,128)(2,1)S(1)}, bf16[2048,128]{1,0:T(8,128)(2,1)S(1)}, u32[]{:S(2)}, u32[]{:S(2)}) collective-permute-start(bf16[2048,128]{1,0:T(8,128)(2,1)S(1)} %get-tuple-element.55), channel_id=1, source_target_pairs={{0,96},{32,0},{64,32},{96,64},{1,97},{33,1},{65,33},{97,65},{2,98}... | collective-permute-start | bytes 1572872 | tf_op jit(solution)/shard_map/ppermute | solution.py:41
  134.9 6.9 %collective-permute-done.27.refs_1_ = bf16[2048,128]{1,0:T(8,128)(2,1)S(1)} collective-permute-done((bf16[2048,128]{1,0:T(8,128)(2,1)S(1)}, bf16[2048,128]{1,0:T(8,128)(2,1)S(1)}, u32[]{:S(2)}, u32[]{:S(2)}) %collective-permute-start.27) | collective-permute-done | bytes 524320 | tf_op jit(solution)/shard_map/ppermute | solution.py:41
  142.1 1.6 collective-permute-done.30.refs_2_
  143.9 3.0 %collective-permute-done.32.refs_5_ = bf16[2048,128]{1,0:T(8,128)(2,1)S(1)} collective-permute-done((bf16[2048,128]{1,0:T(8,128)(2,1)S(1)}, bf16[2048,128]{1,0:T(8,128)(2,1)S(1)}, u32[]{:S(2)}, u32[]{:S(2)}) %collective-permute-start.32) | collective-permute-done | bytes 524320 | tf_op jit(solution)/shard_map/ppermute | solution.py:41
  147.9 4.8 %collective-permute-done.26.refs_2_ = bf16[2048,128]{1,0:T(8,128)(2,1)S(1)} collective-permute-done((bf16[2048,128]{1,0:T(8,128)(2,1)S(1)}, bf16[2048,128]{1,0:T(8,128)(2,1)S(1)}, u32[]{:S(2)}, u32[]{:S(2)}) %collective-permute-start.26) | collective-permute-done | bytes 524320 | tf_op jit(solution)/shard_map/ppermute | solution.py:41
  152.6 2.1 collective-permute-start.36
  155.3 3.2 %collective-permute-done.33.refs_3_ = bf16[2048,128]{1,0:T(8,128)(2,1)S(1)} collective-permute-done((bf16[2048,128]{1,0:T(8,128)(2,1)S(1)}, bf16[2048,128]{1,0:T(8,128)(2,1)S(1)}, u32[]{:S(2)}, u32[]{:S(2)}) %collective-permute-start.33) | collective-permute-done | bytes 524320 | tf_op jit(solution)/shard_map/ppermute | solution.py:41
  158.5 11.4 %collective-permute-done.36.refs_7_ = bf16[2048,128]{1,0:T(8,128)(2,1)S(1)} collective-permute-done((bf16[2048,128]{1,0:T(8,128)(2,1)S(1)}, bf16[2048,128]{1,0:T(8,128)(2,1)S(1)}, u32[]{:S(2)}, u32[]{:S(2)}) %collective-permute-start.36) | collective-permute-done | bytes 524320 | tf_op jit(solution)/shard_map/ppermute | solution.py:41
  169.9 2.5 %shard_map.57 = (f32[2048,256]{1,0:T(8,128)}, f32[8,256]{1,0:T(8,128)S(1)}) custom-call(bf16[2048,256]{1,0:T(8,128)(2,1)S(1)} %bitcast.30, f32[8,256]{1,0:T(8,128)S(1)} %shard_map.49.mine_ref, f32[8,256]{1,0:T(8,128)S(1)} %collective-permute-done.other_ref, f32[8,128]{1,0:T(8,128)S(1)} %get-tuple-element.37.diag_ref, ...), custom_call_target="tpu_custom_call" | custom-call | bytes 7368704 | tf_op jit(solution)/shard_map/pallas_call | solution.py:24
  172.4 1.2 collective-permute-done.37.s_other
  173.6 1.6 copy-done.1
  175.1 1.5 shard_map.58
  176.7 6.9 %all-to-all-start.1 = ((bf16[64,32,256]{2,1,0:T(8,128)(2,1)}), bf16[64,32,256]{2,1,0:T(8,128)(2,1)S(1)}, u32[]{:S(2)}, u32[]{:S(2)}) async-start(bf16[64,32,256]{2,1,0:T(8,128)(2,1)} %bitcast.3), calls=%async_computation.1 | async-start | bytes 2097152 | tf_op jit(solution)/shard_map/all_to_all | solution.py:267
  183.6 1.7 collective-permute-start.17
  185.2 11.5 %collective-permute-done.17 = f32[8,128]{1,0:T(8,128)S(1)} collective-permute-done((f32[8,128]{1,0:T(8,128)S(1)}, f32[8,128]{1,0:T(8,128)S(1)}, u32[]{:S(2)}, u32[]{:S(2)}) %collective-permute-start.17) | collective-permute-done | bytes 4128 | tf_op jit(solution)/shard_map/ppermute | solution.py:45
  196.8 2.7 %collective-permute-start.18 = (f32[8,128]{1,0:T(8,128)S(1)}, f32[8,128]{1,0:T(8,128)S(1)}, u32[]{:S(2)}, u32[]{:S(2)}) collective-permute-start(f32[8,128]{1,0:T(8,128)S(1)} %add.18), channel_id=1, source_target_pairs={{0,16},{16,0},{1,17},{17,1},{2,18},{18,2},{3,19},{19,3},{4,20},{20... | collective-permute-start | bytes 12296 | tf_op jit(solution)/shard_map/ppermute | solution.py:45
  199.5 2.4 %collective-permute-done.18 = f32[8,128]{1,0:T(8,128)S(1)} collective-permute-done((f32[8,128]{1,0:T(8,128)S(1)}, f32[8,128]{1,0:T(8,128)S(1)}, u32[]{:S(2)}, u32[]{:S(2)}) %collective-permute-start.18) | collective-permute-done | bytes 4128 | tf_op jit(solution)/shard_map/ppermute | solution.py:45
  201.9 1.5 collective-permute-start.19
  203.4 2.1 collective-permute-done.19
  205.5 3.0 %collective-permute-start.20 = (f32[8,128]{1,0:T(8,128)S(1)}, f32[8,128]{1,0:T(8,128)S(1)}, u32[]{:S(2)}, u32[]{:S(2)}) collective-permute-start(f32[8,128]{1,0:T(8,128)S(1)} %add.20), channel_id=1, source_target_pairs={{0,4},{2,6},{4,0},{6,2},{1,5},{3,7},{5,1},{7,3},{8,12},{10,14},{12... | collective-permute-start | bytes 12296 | tf_op jit(solution)/shard_map/ppermute | solution.py:45
  208.5 2.1 collective-permute-done.20
  210.6 1.5 collective-permute-start.21
  212.1 2.1 collective-permute-done.21
  214.2 3.1 %collective-permute-start.22 = (f32[8,128]{1,0:T(8,128)S(1)}, f32[8,128]{1,0:T(8,128)S(1)}, u32[]{:S(2)}, u32[]{:S(2)}) collective-permute-start(f32[8,128]{1,0:T(8,128)S(1)} %add.22), channel_id=1, source_target_pairs={{0,64},{32,96},{64,0},{96,32},{1,65},{33,97},{65,1},{97,33},{2,66}... | collective-permute-start | bytes 12296 | tf_op jit(solution)/shard_map/ppermute | solution.py:45
  217.3 2.0 collective-permute-done.22
  (90 shorter events, 13.3 us)
Async XLA Ops:
  33.7 1.2 collective-permute-start
  35.4 61.6 %copy-start.3 = (bf16[2048,128]{1,0:T(8,128)(2,1)}, bf16[2048,128]{1,0:T(8,128)(2,1)S(1)}, u32[]{:S(2)}) copy-start(bf16[2048,128]{1,0:T(8,128)(2,1)S(1)} %get-tuple-element.34.refs_8_) | copy-start | bytes 1572868
  35.4 66.1 %copy-start.2 = (bf16[2048,128]{1,0:T(8,128)(2,1)}, bf16[2048,128]{1,0:T(8,128)(2,1)S(1)}, u32[]{:S(2)}) copy-start(bf16[2048,128]{1,0:T(8,128)(2,1)S(1)} %get-tuple-element.33.refs_0_) | copy-start | bytes 1572868
  35.4 14.8 %collective-permute-start.1 = (bf16[2048,128]{1,0:T(8,128)(2,1)S(1)}, bf16[2048,128]{1,0:T(8,128)(2,1)S(1)}, u32[]{:S(2)}, u32[]{:S(2)}) collective-permute-start(bf16[2048,128]{1,0:T(8,128)(2,1)S(1)} %get-tuple-element.33.refs_0_), channel_id=1, source_target_pairs={{0,8},{8,0},{1,9},{9,1},{2,10},{10,2},{3,11},{11,3},{4,12},{12,4},... | collective-permute-start | bytes 1572872 | tf_op jit(solution)/shard_map/ppermute | solution.py:41
  36.1 14.9 %collective-permute-start.2 = (bf16[2048,128]{1,0:T(8,128)(2,1)S(1)}, bf16[2048,128]{1,0:T(8,128)(2,1)S(1)}, u32[]{:S(2)}, u32[]{:S(2)}) collective-permute-start(bf16[2048,128]{1,0:T(8,128)(2,1)S(1)} %get-tuple-element.33.refs_0_), channel_id=1, source_target_pairs={{0,2},{2,4},{4,6},{6,0},{1,3},{3,5},{5,7},{7,1},{8,10},{10,12},{12... | collective-permute-start | bytes 1572872 | tf_op jit(solution)/shard_map/ppermute | solution.py:41
  36.7 15.1 %collective-permute-start.4 = (bf16[2048,128]{1,0:T(8,128)(2,1)S(1)}, bf16[2048,128]{1,0:T(8,128)(2,1)S(1)}, u32[]{:S(2)}, u32[]{:S(2)}) collective-permute-start(bf16[2048,128]{1,0:T(8,128)(2,1)S(1)} %get-tuple-element.33.refs_0_), channel_id=1, source_target_pairs={{0,6},{2,0},{4,2},{6,4},{1,7},{3,1},{5,3},{7,5},{8,14},{10,8},{12,... | collective-permute-start | bytes 1572872 | tf_op jit(solution)/shard_map/ppermute | solution.py:41
  39.3 21.4 %collective-permute-start.8 = (bf16[2048,128]{1,0:T(8,128)(2,1)S(1)}, bf16[2048,128]{1,0:T(8,128)(2,1)S(1)}, u32[]{:S(2)}, u32[]{:S(2)}) collective-permute-start(bf16[2048,128]{1,0:T(8,128)(2,1)S(1)} %get-tuple-element.34.refs_8_), channel_id=1, source_target_pairs={{0,16},{16,0},{1,17},{17,1},{2,18},{18,2},{3,19},{19,3},{4,20},{20... | collective-permute-start | bytes 1572872 | tf_op jit(solution)/shard_map/ppermute | solution.py:41
  40.8 20.0 %collective-permute-start.9 = (bf16[2048,128]{1,0:T(8,128)(2,1)S(1)}, bf16[2048,128]{1,0:T(8,128)(2,1)S(1)}, u32[]{:S(2)}, u32[]{:S(2)}) collective-permute-start(bf16[2048,128]{1,0:T(8,128)(2,1)S(1)} %get-tuple-element.34.refs_8_), channel_id=1, source_target_pairs={{0,32},{32,64},{64,96},{96,0},{1,33},{33,65},{65,97},{97,1},{2,34}... | collective-permute-start | bytes 1572872 | tf_op jit(solution)/shard_map/ppermute | solution.py:41
  50.3 51.2 %copy-start.4 = (bf16[2048,128]{1,0:T(8,128)(2,1)}, bf16[2048,128]{1,0:T(8,128)(2,1)S(1)}, u32[]{:S(2)}) copy-start(bf16[2048,128]{1,0:T(8,128)(2,1)S(1)} %collective-permute-done.1.refs_1_) | copy-start | bytes 1572868
  50.3 13.7 %collective-permute-start.11 = (bf16[2048,128]{1,0:T(8,128)(2,1)S(1)}, bf16[2048,128]{1,0:T(8,128)(2,1)S(1)}, u32[]{:S(2)}, u32[]{:S(2)}) collective-permute-start(bf16[2048,128]{1,0:T(8,128)(2,1)S(1)} %get-tuple-element.34.refs_8_), channel_id=1, source_target_pairs={{0,96},{32,0},{64,32},{96,64},{1,97},{33,1},{65,33},{97,65},{2,98}... | collective-permute-start | bytes 1572872 | tf_op jit(solution)/shard_map/ppermute | solution.py:41
  51.0 50.5 %copy-start.5 = (bf16[2048,128]{1,0:T(8,128)(2,1)}, bf16[2048,128]{1,0:T(8,128)(2,1)S(1)}, u32[]{:S(2)}) copy-start(bf16[2048,128]{1,0:T(8,128)(2,1)S(1)} %collective-permute-done.2.refs_2_) | copy-start | bytes 1572868
  51.0 14.2 %collective-permute-start.3 = (bf16[2048,128]{1,0:T(8,128)(2,1)S(1)}, bf16[2048,128]{1,0:T(8,128)(2,1)S(1)}, u32[]{:S(2)}, u32[]{:S(2)}) collective-permute-start(bf16[2048,128]{1,0:T(8,128)(2,1)S(1)} %collective-permute-done.1.refs_1_), channel_id=1, source_target_pairs={{0,2},{2,4},{4,6},{6,0},{1,3},{3,5},{5,7},{7,1},{8,10},{10,12},{12... | collective-permute-start | bytes 1572872 | tf_op jit(solution)/shard_map/ppermute | solution.py:41
  51.8 49.7 %copy-start.6 = (bf16[2048,128]{1,0:T(8,128)(2,1)}, bf16[2048,128]{1,0:T(8,128)(2,1)S(1)}, u32[]{:S(2)}) copy-start(bf16[2048,128]{1,0:T(8,128)(2,1)S(1)} %collective-permute-done.4.refs_4_) | copy-start | bytes 1572868
  51.8 14.1 %collective-permute-start.5 = (bf16[2048,128]{1,0:T(8,128)(2,1)S(1)}, bf16[2048,128]{1,0:T(8,128)(2,1)S(1)}, u32[]{:S(2)}, u32[]{:S(2)}) collective-permute-start(bf16[2048,128]{1,0:T(8,128)(2,1)S(1)} %collective-permute-done.1.refs_1_), channel_id=1, source_target_pairs={{0,6},{2,0},{4,2},{6,4},{1,7},{3,1},{5,3},{7,5},{8,14},{10,8},{12,... | collective-permute-start | bytes 1572872 | tf_op jit(solution)/shard_map/ppermute | solution.py:41
  60.7 36.3 %copy-start.7 = (bf16[2048,128]{1,0:T(8,128)(2,1)}, bf16[2048,128]{1,0:T(8,128)(2,1)S(1)}, u32[]{:S(2)}) copy-start(bf16[2048,128]{1,0:T(8,128)(2,1)S(1)} %collective-permute-done.8.refs_9_) | copy-start | bytes 1572868
  60.7 14.4 %collective-permute-start.10 = (bf16[2048,128]{1,0:T(8,128)(2,1)S(1)}, bf16[2048,128]{1,0:T(8,128)(2,1)S(1)}, u32[]{:S(2)}, u32[]{:S(2)}) collective-permute-start(bf16[2048,128]{1,0:T(8,128)(2,1)S(1)} %collective-permute-done.8.refs_9_), channel_id=1, source_target_pairs={{0,32},{32,64},{64,96},{96,0},{1,33},{33,65},{65,97},{97,1},{2,34}... | collective-permute-start | bytes 1572872 | tf_op jit(solution)/shard_map/ppermute | solution.py:41
  60.8 36.3 %copy-start.8 = (bf16[2048,128]{1,0:T(8,128)(2,1)}, bf16[2048,128]{1,0:T(8,128)(2,1)S(1)}, u32[]{:S(2)}) copy-start(bf16[2048,128]{1,0:T(8,128)(2,1)S(1)} %collective-permute-done.9.refs_10_) | copy-start | bytes 1572868
  60.8 15.8 %collective-permute-start.12 = (bf16[2048,128]{1,0:T(8,128)(2,1)S(1)}, bf16[2048,128]{1,0:T(8,128)(2,1)S(1)}, u32[]{:S(2)}, u32[]{:S(2)}) collective-permute-start(bf16[2048,128]{1,0:T(8,128)(2,1)S(1)} %collective-permute-done.8.refs_9_), channel_id=1, source_target_pairs={{0,96},{32,0},{64,32},{96,64},{1,97},{33,1},{65,33},{97,65},{2,98}... | collective-permute-start | bytes 1572872 | tf_op jit(solution)/shard_map/ppermute | solution.py:41
  64.0 12.6 %collective-permute-start.6 = (bf16[2048,128]{1,0:T(8,128)(2,1)S(1)}, bf16[2048,128]{1,0:T(8,128)(2,1)S(1)}, u32[]{:S(2)}, u32[]{:S(2)}) collective-permute-start(bf16[2048,128]{1,0:T(8,128)(2,1)S(1)} %collective-permute-done.4.refs_4_), channel_id=1, source_target_pairs={{0,6},{2,0},{4,2},{6,4},{1,7},{3,1},{5,3},{7,5},{8,14},{10,8},{12,... | collective-permute-start | bytes 1572872 | tf_op jit(solution)/shard_map/ppermute | solution.py:41
  65.3 36.3 %copy-start.9 = (bf16[2048,128]{1,0:T(8,128)(2,1)}, bf16[2048,128]{1,0:T(8,128)(2,1)S(1)}, u32[]{:S(2)}) copy-start(bf16[2048,128]{1,0:T(8,128)(2,1)S(1)} %collective-permute-done.3.refs_3_) | copy-start | bytes 1572868
  65.3 20.4 %collective-permute-start.13 = (bf16[2048,128]{1,0:T(8,128)(2,1)S(1)}, bf16[2048,128]{1,0:T(8,128)(2,1)S(1)}, u32[]{:S(2)}, u32[]{:S(2)}) collective-permute-start(bf16[2048,128]{1,0:T(8,128)(2,1)S(1)} %collective-permute-done.11.refs_12_), channel_id=1, source_target_pairs={{0,96},{32,0},{64,32},{96,64},{1,97},{33,1},{65,33},{97,65},{2,98}... | collective-permute-start | bytes 1572872 | tf_op jit(solution)/shard_map/ppermute | solution.py:41
  65.8 35.7 %copy-start.10 = (bf16[2048,128]{1,0:T(8,128)(2,1)}, bf16[2048,128]{1,0:T(8,128)(2,1)S(1)}, u32[]{:S(2)}) copy-start(bf16[2048,128]{1,0:T(8,128)(2,1)S(1)} %collective-permute-done.5.refs_5_) | copy-start | bytes 1572868
  65.8 19.8 %collective-permute-start.7 = (bf16[2048,128]{1,0:T(8,128)(2,1)S(1)}, bf16[2048,128]{1,0:T(8,128)(2,1)S(1)}, u32[]{:S(2)}, u32[]{:S(2)}) collective-permute-start(bf16[2048,128]{1,0:T(8,128)(2,1)S(1)} %collective-permute-done.3.refs_3_), channel_id=1, source_target_pairs={{0,2},{2,4},{4,6},{6,0},{1,3},{3,5},{5,7},{7,1},{8,10},{10,12},{12... | collective-permute-start | bytes 1572872 | tf_op jit(solution)/shard_map/ppermute | solution.py:41
  75.1 13.5 %collective-permute-start.14 = (bf16[2048,128]{1,0:T(8,128)(2,1)S(1)}, bf16[2048,128]{1,0:T(8,128)(2,1)S(1)}, u32[]{:S(2)}, u32[]{:S(2)}) collective-permute-start(bf16[2048,128]{1,0:T(8,128)(2,1)S(1)} %collective-permute-done.10.refs_11_), channel_id=1, source_target_pairs={{0,32},{32,64},{64,96},{96,0},{1,33},{33,65},{65,97},{97,1},{2,34}... | collective-permute-start | bytes 1572872 | tf_op jit(solution)/shard_map/ppermute | solution.py:41
  97.0 4.5 %collective-permute-start.15 = (bf16[1024,1024]{1,0:T(8,128)(2,1)}, bf16[1024,1024]{1,0:T(8,128)(2,1)S(1)}, u32[]{:S(2)}, u32[]{:S(2)}) collective-permute-start(bf16[1024,1024]{1,0:T(8,128)(2,1)} %shard_map.51.refs_16_), channel_id=1, source_target_pairs={{0,1},{1,0},{2,3},{3,2},{4,5},{5,4},{6,7},{7,6},{8,9},{9,8},{10,11... | collective-permute-start | bytes 6291464 | tf_op jit(solution)/shard_map/ppermute | solution.py:41
  97.1 3.9 %collective-permute-start.16 = (f32[8,128]{1,0:T(8,128)S(1)}, f32[8,128]{1,0:T(8,128)S(1)}, u32[]{:S(2)}, u32[]{:S(2)}) collective-permute-start(f32[8,128]{1,0:T(8,128)S(1)} %get-tuple-element.35.refs_18_), channel_id=1, source_target_pairs={{0,1},{1,0},{2,3},{3,2},{4,5},{5,4},{6,7},{7,6},{8,9},{9,8},{10,11... | collective-permute-start | bytes 12296 | tf_op jit(solution)/shard_map/ppermute | solution.py:41
  110.4 20.9 %collective-permute-start.23 = (bf16[2048,128]{1,0:T(8,128)(2,1)S(1)}, bf16[2048,128]{1,0:T(8,128)(2,1)S(1)}, u32[]{:S(2)}, u32[]{:S(2)}) collective-permute-start(bf16[2048,128]{1,0:T(8,128)(2,1)S(1)} %get-tuple-element.41), channel_id=1, source_target_pairs={{0,2},{2,4},{4,6},{6,0},{1,3},{3,5},{5,7},{7,1},{8,10},{10,12},{12... | collective-permute-start | bytes 1572872 | tf_op jit(solution)/shard_map/ppermute | solution.py:41
  110.9 23.6 %collective-permute-start.24 = (bf16[2048,128]{1,0:T(8,128)(2,1)S(1)}, bf16[2048,128]{1,0:T(8,128)(2,1)S(1)}, u32[]{:S(2)}, u32[]{:S(2)}) collective-permute-start(bf16[2048,128]{1,0:T(8,128)(2,1)S(1)} %get-tuple-element.43), channel_id=1, source_target_pairs={{0,32},{32,64},{64,96},{96,0},{1,33},{33,65},{65,97},{97,1},{2,34}... | collective-permute-start | bytes 1572872 | tf_op jit(solution)/shard_map/ppermute | solution.py:41
  110.9 16.9 %collective-permute-start.28 = (bf16[2048,128]{1,0:T(8,128)(2,1)S(1)}, bf16[2048,128]{1,0:T(8,128)(2,1)S(1)}, u32[]{:S(2)}, u32[]{:S(2)}) collective-permute-start(bf16[2048,128]{1,0:T(8,128)(2,1)S(1)} %get-tuple-element.49), channel_id=1, source_target_pairs={{0,6},{2,0},{4,2},{6,4},{1,7},{3,1},{5,3},{7,5},{8,14},{10,8},{12,... | collective-permute-start | bytes 1572872 | tf_op jit(solution)/shard_map/ppermute | solution.py:41
  113.6 14.2 %collective-permute-start.29 = (bf16[2048,128]{1,0:T(8,128)(2,1)S(1)}, bf16[2048,128]{1,0:T(8,128)(2,1)S(1)}, u32[]{:S(2)}, u32[]{:S(2)}) collective-permute-start(bf16[2048,128]{1,0:T(8,128)(2,1)S(1)} %get-tuple-element.51), channel_id=1, source_target_pairs={{0,96},{32,0},{64,32},{96,64},{1,97},{33,1},{65,33},{97,65},{2,98}... | collective-permute-start | bytes 1572872 | tf_op jit(solution)/shard_map/ppermute | solution.py:41
  127.7 14.1 %collective-permute-start.27 = (bf16[2048,128]{1,0:T(8,128)(2,1)S(1)}, bf16[2048,128]{1,0:T(8,128)(2,1)S(1)}, u32[]{:S(2)}, u32[]{:S(2)}) collective-permute-start(bf16[2048,128]{1,0:T(8,128)(2,1)S(1)} %get-tuple-element.47), channel_id=1, source_target_pairs={{0,2},{2,4},{4,6},{6,0},{1,3},{3,5},{5,7},{7,1},{8,10},{10,12},{12... | collective-permute-start | bytes 1572872 | tf_op jit(solution)/shard_map/ppermute | solution.py:41
  127.8 14.3 %collective-permute-start.31 = (bf16[2048,128]{1,0:T(8,128)(2,1)}, bf16[2048,128]{1,0:T(8,128)(2,1)S(1)}, u32[]{:S(2)}, u32[]{:S(2)}) collective-permute-start(bf16[2048,128]{1,0:T(8,128)(2,1)} %get-tuple-element.54), channel_id=1, source_target_pairs={{0,32},{32,64},{64,96},{96,0},{1,33},{33,65},{65,97},{97,1},{2,34}... | collective-permute-start | bytes 1572872 | tf_op jit(solution)/shard_map/ppermute | solution.py:41
  128.1 15.6 %collective-permute-start.30 = (bf16[2048,128]{1,0:T(8,128)(2,1)S(1)}, bf16[2048,128]{1,0:T(8,128)(2,1)S(1)}, u32[]{:S(2)}, u32[]{:S(2)}) collective-permute-start(bf16[2048,128]{1,0:T(8,128)(2,1)S(1)} %get-tuple-element.52), channel_id=1, source_target_pairs={{0,6},{2,0},{4,2},{6,4},{1,7},{3,1},{5,3},{7,5},{8,14},{10,8},{12,... | collective-permute-start | bytes 1572872 | tf_op jit(solution)/shard_map/ppermute | solution.py:41
  131.3 15.6 %collective-permute-start.32 = (bf16[2048,128]{1,0:T(8,128)(2,1)S(1)}, bf16[2048,128]{1,0:T(8,128)(2,1)S(1)}, u32[]{:S(2)}, u32[]{:S(2)}) collective-permute-start(bf16[2048,128]{1,0:T(8,128)(2,1)S(1)} %get-tuple-element.55), channel_id=1, source_target_pairs={{0,96},{32,0},{64,32},{96,64},{1,97},{33,1},{65,33},{97,65},{2,98}... | collective-permute-start | bytes 1572872 | tf_op jit(solution)/shard_map/ppermute | solution.py:41
  134.6 18.1 %collective-permute-start.26 = (bf16[2048,128]{1,0:T(8,128)(2,1)S(1)}, bf16[2048,128]{1,0:T(8,128)(2,1)S(1)}, u32[]{:S(2)}, u32[]{:S(2)}) collective-permute-start(bf16[2048,128]{1,0:T(8,128)(2,1)S(1)} %get-tuple-element.45), channel_id=1, source_target_pairs={{0,6},{2,0},{4,2},{6,4},{1,7},{3,1},{5,3},{7,5},{8,14},{10,8},{12,... | collective-permute-start | bytes 1572872 | tf_op jit(solution)/shard_map/ppermute | solution.py:41
  141.8 13.5 %collective-permute-start.35 = (bf16[2048,128]{1,0:T(8,128)(2,1)S(1)}, bf16[2048,128]{1,0:T(8,128)(2,1)S(1)}, u32[]{:S(2)}, u32[]{:S(2)}) collective-permute-start(bf16[2048,128]{1,0:T(8,128)(2,1)S(1)} %get-tuple-element.59), channel_id=1, source_target_pairs={{0,96},{32,0},{64,32},{96,64},{1,97},{33,1},{65,33},{97,65},{2,98}... | collective-permute-start | bytes 1572872 | tf_op jit(solution)/shard_map/ppermute | solution.py:41
  142.1 13.2 %collective-permute-start.25 = (bf16[2048,128]{1,0:T(8,128)(2,1)S(1)}, bf16[2048,128]{1,0:T(8,128)(2,1)S(1)}, u32[]{:S(2)}, u32[]{:S(2)}) collective-permute-start(bf16[2048,128]{1,0:T(8,128)(2,1)S(1)} %get-tuple-element.44), channel_id=1, source_target_pairs={{0,2},{2,4},{4,6},{6,0},{1,3},{3,5},{5,7},{7,1},{8,10},{10,12},{12... | collective-permute-start | bytes 1572872 | tf_op jit(solution)/shard_map/ppermute | solution.py:41
  143.7 11.6 %collective-permute-start.34 = (bf16[2048,128]{1,0:T(8,128)(2,1)S(1)}, bf16[2048,128]{1,0:T(8,128)(2,1)S(1)}, u32[]{:S(2)}, u32[]{:S(2)}) collective-permute-start(bf16[2048,128]{1,0:T(8,128)(2,1)S(1)} %get-tuple-element.58), channel_id=1, source_target_pairs={{0,32},{32,64},{64,96},{96,0},{1,33},{33,65},{65,97},{97,1},{2,34}... | collective-permute-start | bytes 1572872 | tf_op jit(solution)/shard_map/ppermute | solution.py:41
  147.3 11.2 %collective-permute-start.33 = (bf16[2048,128]{1,0:T(8,128)(2,1)S(1)}, bf16[2048,128]{1,0:T(8,128)(2,1)S(1)}, u32[]{:S(2)}, u32[]{:S(2)}) collective-permute-start(bf16[2048,128]{1,0:T(8,128)(2,1)S(1)} %get-tuple-element.56), channel_id=1, source_target_pairs={{0,8},{8,0},{1,9},{9,1},{2,10},{10,2},{3,11},{11,3},{4,12},{12,4},... | collective-permute-start | bytes 1572872 | tf_op jit(solution)/shard_map/ppermute | solution.py:41
  152.6 17.3 %collective-permute-start.36 = (bf16[2048,128]{1,0:T(8,128)(2,1)S(1)}, bf16[2048,128]{1,0:T(8,128)(2,1)S(1)}, u32[]{:S(2)}, u32[]{:S(2)}) collective-permute-start(bf16[2048,128]{1,0:T(8,128)(2,1)S(1)} %get-tuple-element.60), channel_id=1, source_target_pairs={{0,16},{16,0},{1,17},{17,1},{2,18},{18,2},{3,19},{19,3},{4,20},{20... | collective-permute-start | bytes 1572872 | tf_op jit(solution)/shard_map/ppermute | solution.py:41
  172.4 1.2 collective-permute-start.37
  176.7 43.9 %all-to-all-start.1 = ((bf16[64,32,256]{2,1,0:T(8,128)(2,1)}), bf16[64,32,256]{2,1,0:T(8,128)(2,1)S(1)}, u32[]{:S(2)}, u32[]{:S(2)}) async-start(bf16[64,32,256]{2,1,0:T(8,128)(2,1)} %bitcast.3), calls=%async_computation.1 | async-start | bytes 2097152 | tf_op jit(solution)/shard_map/all_to_all | solution.py:267
  183.6 13.2 %collective-permute-start.17 = (f32[8,128]{1,0:T(8,128)S(1)}, f32[8,128]{1,0:T(8,128)S(1)}, u32[]{:S(2)}, u32[]{:S(2)}) collective-permute-start(f32[8,128]{1,0:T(8,128)S(1)} %get-tuple-element.36), channel_id=1, source_target_pairs={{0,8},{8,0},{1,9},{9,1},{2,10},{10,2},{3,11},{11,3},{4,12},{12,4},... | collective-permute-start | bytes 12296 | tf_op jit(solution)/shard_map/ppermute | solution.py:45
  196.8 5.1 %collective-permute-start.18 = (f32[8,128]{1,0:T(8,128)S(1)}, f32[8,128]{1,0:T(8,128)S(1)}, u32[]{:S(2)}, u32[]{:S(2)}) collective-permute-start(f32[8,128]{1,0:T(8,128)S(1)} %add.18), channel_id=1, source_target_pairs={{0,16},{16,0},{1,17},{17,1},{2,18},{18,2},{3,19},{19,3},{4,20},{20... | collective-permute-start | bytes 12296 | tf_op jit(solution)/shard_map/ppermute | solution.py:45
  201.9 3.6 %collective-permute-start.19 = (f32[8,128]{1,0:T(8,128)S(1)}, f32[8,128]{1,0:T(8,128)S(1)}, u32[]{:S(2)}, u32[]{:S(2)}) collective-permute-start(f32[8,128]{1,0:T(8,128)S(1)} %add.19), channel_id=1, source_target_pairs={{0,2},{2,0},{4,6},{6,4},{1,3},{3,1},{5,7},{7,5},{8,10},{10,8},{12,... | collective-permute-start | bytes 12296 | tf_op jit(solution)/shard_map/ppermute | solution.py:45
  205.5 5.1 %collective-permute-start.20 = (f32[8,128]{1,0:T(8,128)S(1)}, f32[8,128]{1,0:T(8,128)S(1)}, u32[]{:S(2)}, u32[]{:S(2)}) collective-permute-start(f32[8,128]{1,0:T(8,128)S(1)} %add.20), channel_id=1, source_target_pairs={{0,4},{2,6},{4,0},{6,2},{1,5},{3,7},{5,1},{7,3},{8,12},{10,14},{12... | collective-permute-start | bytes 12296 | tf_op jit(solution)/shard_map/ppermute | solution.py:45
  210.6 3.6 %collective-permute-start.21 = (f32[8,128]{1,0:T(8,128)S(1)}, f32[8,128]{1,0:T(8,128)S(1)}, u32[]{:S(2)}, u32[]{:S(2)}) collective-permute-start(f32[8,128]{1,0:T(8,128)S(1)} %add.21), channel_id=1, source_target_pairs={{0,32},{32,0},{64,96},{96,64},{1,33},{33,1},{65,97},{97,65},{2,34}... | collective-permute-start | bytes 12296 | tf_op jit(solution)/shard_map/ppermute | solution.py:45
  214.2 5.1 %collective-permute-start.22 = (f32[8,128]{1,0:T(8,128)S(1)}, f32[8,128]{1,0:T(8,128)S(1)}, u32[]{:S(2)}, u32[]{:S(2)}) collective-permute-start(f32[8,128]{1,0:T(8,128)S(1)} %add.22), channel_id=1, source_target_pairs={{0,64},{32,96},{64,0},{96,32},{1,65},{33,97},{65,1},{97,33},{2,66}... | collective-permute-start | bytes 12296 | tf_op jit(solution)/shard_map/ppermute | solution.py:45
  (10 other events, 94.2 us)
